TPU v7x, 32 devices: a whole 2x2x4 slice. The times are simulated.
32 devices in a mesh: dp: 4 (over x, core), ctx: 8 (over z, y).
Axes of the slice: x: 2, y: 2, z: 4, core: 2. Of those that a mesh axis runs over, the one named last changes fastest.
Arguments:
- queries: bfloat16 [4, 3072, 1536], P('dp', 'ctx'), may hold values from -160 to 160
- key_rows: bfloat16 [4, 3072, 1536], P('dp', 'ctx'), may hold values from -8 to 8
- value_rows: bfloat16 [4, 3072, 1536], P('dp', 'ctx'), may hold values from -6 to 6
- tile_lists: int32 [4, 8, 5], P('dp', 'ctx'), may hold values from 0 to 7, as said below
- tile_counts: int32 [4, 8], P('dp', 'ctx'), may hold values from 1 to 5
- out_weight: bfloat16 [1536, 1536], P('dp'), may hold values from -0.15625 to 0.15625
Outputs:
- projected: bfloat16 [4, 3072, 1536], P('dp', 'ctx')
Inputs may be any that keep to these rules, and one draw needn't show every extreme that they name: For s < tile_counts[b, t], tile_lists[b, t, s] are distinct tiles of the video within 2 of t, increasing, and t is among them; later slots hold t.
All inputs are finite; a program needn't handle non-finite values.
Results may differ from a plain program's by a relative error of at most 0.0056.
Values may be sent and summed in bfloat16 or wider, within the bound.
A program may use at most 64 MiB of HBM per device.

v0:
```python
import math

import jax
import jax.numpy as jnp
from jax import lax
from jax.sharding import PartitionSpec as P

HEADS = 12
HD = 128
DOUT = 1536
REACH = 2
SLOTS = 5


def from_behind(value, axis, by):
    size = lax.axis_size(axis)
    pairs = [(i, i + by) for i in range(size) if 0 <= i + by < size]
    return lax.ppermute(value, axis, pairs)


def masked_video(query_block, key_window, value_window, visible_tiles):
    tok_rows = query_block.shape[0]
    expanded = (jnp.repeat(visible_tiles, tok_rows) > 0)[None, :]

    def per_head(head_pos):
        start_col = head_pos * HD
        query_head = lax.dynamic_slice_in_dim(query_block, start_col, HD, 1)
        key_head = lax.dynamic_slice_in_dim(key_window, start_col, HD, 1)
        value_head = lax.dynamic_slice_in_dim(value_window, start_col, HD, 1)
        scores = jnp.einsum(
            "td,kd->tk", query_head, key_head, preferred_element_type=jnp.float32
        ) * (1.0 / math.sqrt(HD))
        peak_rows = jnp.max(jnp.where(expanded, scores, jnp.float32(-1e30)), axis=1, keepdims=True)
        exponent = jnp.where(expanded, jnp.exp(scores - peak_rows), jnp.float32(0.0))
        totals = jnp.sum(exponent, axis=1, keepdims=True)
        mixture = jnp.dot(
            exponent.astype(jnp.bfloat16), value_head, preferred_element_type=jnp.float32
        )
        return (mixture / totals).astype(jnp.bfloat16)

    per_heads = lax.map(per_head, jnp.arange(HEADS, dtype=jnp.int32))
    return per_heads.transpose(1, 0, 2).reshape(tok_rows, HEADS * HD)


def per_device(queries, key_rows, value_rows, tile_lists, tile_counts, out_weight):
    videos = queries.shape[0]
    tok_rows = queries.shape[1]
    channels = queries.shape[2]
    tile_here = lax.axis_index("ctx")
    key_value = jnp.stack([key_rows, value_rows])
    below_parts = [from_behind(key_value, "ctx", distance) for distance in range(REACH, 0, -1)]
    above_parts = [from_behind(key_value, "ctx", -distance) for distance in range(1, REACH + 1)]
    windowed = jnp.concatenate(below_parts + [key_value] + above_parts, axis=2)
    offsets = jnp.arange(SLOTS, dtype=jnp.int32) - REACH
    in_use = jnp.arange(SLOTS, dtype=jnp.int32)[None, :] < tile_counts[:, 0][:, None]
    matches = (tile_lists[:, 0, :, None] == (tile_here + offsets)[None, None, :]) & in_use[
        :, :, None
    ]
    visible = jnp.any(matches, axis=1).astype(jnp.int32)
    attended = [masked_video(queries[0], windowed[0, 0], windowed[1, 0], visible[0])]
    attention = jnp.stack(attended).reshape(videos * tok_rows, channels)
    projected = jnp.dot(
        attention,
        lax.all_gather(out_weight, "dp", axis=0, tiled=True),
        preferred_element_type=jnp.float32,
    )
    return projected.astype(jnp.bfloat16).reshape(videos, tok_rows, DOUT)


def solution(mesh):
    in_specs = (
        P("dp", "ctx", None),
        P("dp", "ctx", None),
        P("dp", "ctx", None),
        P("dp", "ctx", None),
        P("dp", "ctx"),
        P("dp", None),
    )
    out_specs = P("dp", "ctx", None)
    return jax.shard_map(
        per_device, mesh=mesh, in_specs=in_specs, out_specs=out_specs, check_vma=False
    )
```

profile of v0, /device:TPU:0, one launch (start us, length us, event | category | flops | bytes accessed | tf_op | source)
XLA Modules:
  0.0 208.2 jit_solution(1951956544712172357)
XLA Ops:
  6.5 1.9 pad_maximum_fusion
  8.4 6.4 %collective-permute-start = (bf16[2,1,384,1536]{3,2,1,0:T(8,128)(2,1)S(1)}, bf16[2,1,384,1536]{3,2,1,0:T(8,128)(2,1)}, u32[]{:S(2)}, u32[]{:S(2)}) collective-permute-start(bf16[2,1,384,1536]{3,2,1,0:T(8,128)(2,1)S(1)} %pad_maximum_fusion), channel_id=1, source_target_pairs={{0,2},{1,3},{2,4},{3,5},{4,6},{5,7},{8,10},{9,11},{10,12},{11,13},... | collective-permute-start | bytes 7077896 | tf_op jit(solution)/shard_map/ppermute | solution.py:18
  14.8 4.8 %collective-permute-start.1 = (bf16[2,1,384,1536]{3,2,1,0:T(8,128)(2,1)S(1)}, bf16[2,1,384,1536]{3,2,1,0:T(8,128)(2,1)}, u32[]{:S(2)}, u32[]{:S(2)}) collective-permute-start(bf16[2,1,384,1536]{3,2,1,0:T(8,128)(2,1)S(1)} %pad_maximum_fusion), channel_id=1, source_target_pairs={{0,1},{1,2},{2,3},{3,4},{4,5},{5,6},{6,7},{8,9},{9,10},{10,11},{11... | collective-permute-start | bytes 7077896 | tf_op jit(solution)/shard_map/ppermute | solution.py:18
  19.6 1.3 collective-permute-start.2
  20.9 1.3 collective-permute-start.3
  23.0 40.8 %collective-permute-done = bf16[2,1,384,1536]{3,2,1,0:T(8,128)(2,1)} collective-permute-done((bf16[2,1,384,1536]{3,2,1,0:T(8,128)(2,1)S(1)}, bf16[2,1,384,1536]{3,2,1,0:T(8,128)(2,1)}, u32[]{:S(2)}, u32[]{:S(2)}) %collective-permute-start) | collective-permute-done | bytes 2359328 | tf_op jit(solution)/shard_map/ppermute | solution.py:18
  63.8 1.8 constant_dynamic-update-slice_fusion.5
  65.7 53.3 %collective-permute-done.1 = bf16[2,1,384,1536]{3,2,1,0:T(8,128)(2,1)} collective-permute-done((bf16[2,1,384,1536]{3,2,1,0:T(8,128)(2,1)S(1)}, bf16[2,1,384,1536]{3,2,1,0:T(8,128)(2,1)}, u32[]{:S(2)}, u32[]{:S(2)}) %collective-permute-start.1) | collective-permute-done | bytes 2359328 | tf_op jit(solution)/shard_map/ppermute | solution.py:18
  118.9 1.8 constant_dynamic-update-slice_fusion.4
  121.0 1.8 constant_dynamic-update-slice_fusion.2
  122.9 1.8 constant_dynamic-update-slice_fusion.1
  124.8 4.7 %slice_bitcast_fusion = (bf16[1920,1536]{1,0:T(8,128)(2,1)}, bf16[1920,1536]{1,0:T(8,128)(2,1)}) fusion(bf16[2,1,1920,1536]{3,2,1,0:T(8,128)(2,1)S(1)} %constant_dynamic-update-slice_fusion.1), kind=kLoop, calls=%fused_computation.20 | loop fusion | bytes 23592960 | tf_op jit(solution)/shard_map/squeeze | solution.py:60
  129.5 66.5 %while.11 = (s32[]{:T(128)}, bf16[12,384,128]{1,2,0:T(8,128)(2,1)S(1)}, s32[12]{0:T(128)S(1)}, bf16[384,1536]{1,0:T(8,128)(2,1)}, bf16[1920,1536]{1,0:T(8,128)(2...) while((s32[]{:T(128)}, ...), condition=%wide.region_4.5_spmd.clone, body=%wide.region_1.4_spmd.clone.sunk | while | flops 384220416 | bytes 10440628 | solution.py:41
  130.8 1.8 select_reduce_fusion.2
  132.6 0.6 fusion.33
  133.2 1.6 fusion.34
  136.3 1.8 select_reduce_fusion.2
  138.1 0.6 fusion.33
  138.7 1.6 fusion.34
  141.9 1.8 select_reduce_fusion.2
  143.7 0.6 fusion.33
  144.3 1.6 fusion.34
  147.4 1.8 select_reduce_fusion.2
  149.2 0.6 fusion.33
  149.8 1.6 fusion.34
  153.0 1.8 select_reduce_fusion.2
  154.7 0.6 fusion.33
  155.4 1.6 fusion.34
  158.5 1.8 select_reduce_fusion.2
  160.3 0.6 fusion.33
  160.9 1.6 fusion.34
  164.1 1.8 select_reduce_fusion.2
  165.8 0.6 fusion.33
  166.4 1.6 fusion.34
  169.6 1.8 select_reduce_fusion.2
  171.4 0.6 fusion.33
  172.0 1.6 fusion.34
  175.1 1.8 select_reduce_fusion.2
  176.9 0.6 fusion.33
  177.5 1.6 fusion.34
  180.7 1.8 select_reduce_fusion.2
  183.1 1.6 fusion.34
  186.2 1.8 select_reduce_fusion.2
  188.0 0.6 fusion.33
  188.6 1.6 fusion.34
  191.8 1.8 select_reduce_fusion.2
  194.2 1.6 fusion.34
  196.0 5.4 %fusion.24 = bf16[1,384,1536]{2,1,0:T(8,128)(2,1)} fusion(bf16[384,1536]{0,1:T(8,128)(2,1)S(1)} %bitcast.30, bf16[1536,1536]{1,0:T(8,128)(2,1)} %all-gather.2.cloned.1.call-done), kind=kOutput, calls=%fused_computation.23 | convolution fusion | flops 1812529152 | bytes 7077888 | tf_op jit(solution)/shard_map/dot_general | solution.py:62
  (80 shorter events, 11.9 us)
Async XLA Ops:
  6.5 189.5 %all-gather.2.cloned.1.call-start = ((), (), s32[]{:S(2)}) async-start(), calls=%async_computation | async-start | bytes 5898240 | tf_op jit(solution)/shard_map/all_gather | solution.py:64
  6.5 16.3 %copy-start.2 = (s32[1,1,5]{2,1,0:T(1,128)S(1)}, s32[1,1,5]{2,1,0:T(1,128)}, u32[]{:S(2)}) copy-start(s32[1,1,5]{2,1,0:T(1,128)} %param.11) | copy-start | bytes 64
  8.4 55.4 %collective-permute-start = (bf16[2,1,384,1536]{3,2,1,0:T(8,128)(2,1)S(1)}, bf16[2,1,384,1536]{3,2,1,0:T(8,128)(2,1)}, u32[]{:S(2)}, u32[]{:S(2)}) collective-permute-start(bf16[2,1,384,1536]{3,2,1,0:T(8,128)(2,1)S(1)} %pad_maximum_fusion), channel_id=1, source_target_pairs={{0,2},{1,3},{2,4},{3,5},{4,6},{5,7},{8,10},{9,11},{10,12},{11,13},... | collective-permute-start | bytes 7077896 | tf_op jit(solution)/shard_map/ppermute | solution.py:18
  14.8 104.2 %collective-permute-start.1 = (bf16[2,1,384,1536]{3,2,1,0:T(8,128)(2,1)S(1)}, bf16[2,1,384,1536]{3,2,1,0:T(8,128)(2,1)}, u32[]{:S(2)}, u32[]{:S(2)}) collective-permute-start(bf16[2,1,384,1536]{3,2,1,0:T(8,128)(2,1)S(1)} %pad_maximum_fusion), channel_id=1, source_target_pairs={{0,1},{1,2},{2,3},{3,4},{4,5},{5,6},{6,7},{8,9},{9,10},{10,11},{11... | collective-permute-start | bytes 7077896 | tf_op jit(solution)/shard_map/ppermute | solution.py:18
  19.6 101.4 %collective-permute-start.2 = (bf16[2,1,384,1536]{3,2,1,0:T(8,128)(2,1)S(1)}, bf16[2,1,384,1536]{3,2,1,0:T(8,128)(2,1)}, u32[]{:S(2)}, u32[]{:S(2)}) collective-permute-start(bf16[2,1,384,1536]{3,2,1,0:T(8,128)(2,1)S(1)} %pad_maximum_fusion), channel_id=1, source_target_pairs={{1,0},{2,1},{3,2},{4,3},{5,4},{6,5},{7,6},{9,8},{10,9},{11,10},{12... | collective-permute-start | bytes 7077896 | tf_op jit(solution)/shard_map/ppermute | solution.py:18
  20.9 102.1 %collective-permute-start.3 = (bf16[2,1,384,1536]{3,2,1,0:T(8,128)(2,1)S(1)}, bf16[2,1,384,1536]{3,2,1,0:T(8,128)(2,1)}, u32[]{:S(2)}, u32[]{:S(2)}) collective-permute-start(bf16[2,1,384,1536]{3,2,1,0:T(8,128)(2,1)S(1)} %pad_maximum_fusion), channel_id=1, source_target_pairs={{2,0},{3,1},{4,2},{5,3},{6,4},{7,5},{10,8},{11,9},{12,10},{13,11},... | collective-permute-start | bytes 7077896 | tf_op jit(solution)/shard_map/ppermute | solution.py:18
  65.6 55.1 %copy-start = (bf16[1,384,1536]{2,1,0:T(8,128)(2,1)S(1)}, bf16[1,384,1536]{2,1,0:T(8,128)(2,1)}, u32[]{:S(2)}) copy-start(bf16[1,384,1536]{2,1,0:T(8,128)(2,1)} %param.10) | copy-start | bytes 3538948
  65.7 55.1 %copy-start.1 = (bf16[1,384,1536]{2,1,0:T(8,128)(2,1)S(1)}, bf16[1,384,1536]{2,1,0:T(8,128)(2,1)}, u32[]{:S(2)}) copy-start(bf16[1,384,1536]{2,1,0:T(8,128)(2,1)} %param.9) | copy-start | bytes 3538948
Sparse Core Ops, SparseCore 0:
  22.3 39.5 all-gather.1
where the time goes:
time: 210 us; the launch traced here: 208 us
  waiting for transfers between devices  94.3 us (45%)
  matrix products  46.3 us (22%)
  local copies, waits for them, and re-layouts  22.2 us (11%)
  between operations  14.2 us (7%)
  starting transfers between devices  13.8 us (7%)
  other arithmetic  9.69 us (5%)
  loops' own time  7.84 us (4%)
    ppermute x4, waiting for transfers between devices, from_behind(): return lax.ppermute(value, axis, pairs)  94.3 us
    dot_general x12, matrix products, per_head(): jnp.einsum('td,kd->tk', query_head, key_head, preferred_element_type=jnp....  21.2 us
    dot_general x12, matrix products, per_head(): jnp.dot(exponent.astype(jnp.bfloat16), value_head, preferred_element_type...  19.7 us
    ppermute x4, starting transfers between devices, from_behind(): return lax.ppermute(value, axis, pairs)  13.8 us
    another operation x1, loops' own time, masked_video(): per_heads = lax.map(per_head, jnp.arange(HEADS, dtype=jnp.int32))  7.84 us
    reduce_sum x12, other arithmetic, per_head(): totals = jnp.sum(exponent, axis=1, keepdims=True)  7.57 us
    dynamic_slice x12, local copies, waits for them, and re-layouts, masked_video(): per_heads = lax.map(per_head, jnp.arange(HEADS, dtype=jnp.int32))  7.37 us
    unnamed x9, local copies, waits for them, and re-layouts  5.47 us
  transfers between devices with their start and end apart: 5, of which 3 were waited for; matrix products, arithmetic and copies ran while one was open for 34% of the time, Pallas kernels for 0%

commit v1 on v0

v1 whole, which is shorter than its diff:
```python
import functools
import math

import jax
import jax.numpy as jnp
from jax import lax
from jax.experimental import pallas as pl
from jax.experimental.pallas import tpu as pltpu
from jax.sharding import PartitionSpec as P

HD = 128
REACH = 2
SLOTS = 5
WINDOW = 6
HIDDEN = -1e30
SHUT = 1e30


def kernel(tiles, q_ref, k_ref, v_ref, vis_ref, out_ref,
           q_held, k_held, v_held, vis_held, done, stage,
           own_sem, vis_sem, pair_send, pair_recv, own_send, pass_send, z_recv, back_send, back_recv):
    half = q_held.shape[1]
    me = lax.axis_index("ctx")
    side = lax.rem(me, 2)
    pair = me + 1 - 2 * side
    has_up = me + 2 < tiles
    has_down = me >= 2
    up, down = me + 2, me - 2
    scale = math.log2(math.e) / math.sqrt(HD)

    def columns(ref, which, c):
        return ref.at[0, :, pl.ds(pl.multiple_of((which * half + c) * HD, HD), HD)]

    def remote(src, dst, send, recv, target):
        return pltpu.make_async_remote_copy(
            src_ref=src, dst_ref=dst, send_sem=send, recv_sem=recv,
            device_id={"ctx": target}, device_id_type=pl.DeviceIdType.MESH,
        )

    def to_pair(c):
        return [
            remote(columns(k_ref, 1 - side, c), k_held.at[2 + side, c], pair_send.at[0, c], pair_recv.at[0, c], pair),
            remote(columns(v_ref, 1 - side, c), v_held.at[2 + side, c], pair_send.at[1, c], pair_recv.at[1, c], pair),
            remote(columns(q_ref, 1 - side, c), q_held.at[side, c], pair_send.at[2, c], pair_recv.at[2, c], pair),
        ]

    def from_pair(c):
        other = 1 - side
        return [
            remote(columns(k_ref, side, c), k_held.at[2 + other, c], pair_send.at[0, c], pair_recv.at[0, c], pair),
            remote(columns(v_ref, side, c), v_held.at[2 + other, c], pair_send.at[1, c], pair_recv.at[1, c], pair),
            remote(columns(q_ref, side, c), q_held.at[other, c], pair_send.at[2, c], pair_recv.at[2, c], pair),
        ]

    def own_out(c, way):
        first, target = ((0, up), (4, down))[way]
        return [
            remote(columns(k_ref, side, c), k_held.at[first + side, c], own_send.at[way, 0, c], z_recv.at[way, 0, 0, c], target),
            remote(columns(v_ref, side, c), v_held.at[first + side, c], own_send.at[way, 1, c], z_recv.at[way, 0, 1, c], target),
        ]

    def pass_on(c, way):
        first, target = ((0, up), (4, down))[way]
        other = 1 - side
        return [
            remote(k_held.at[2 + other, c], k_held.at[first + other, c], pass_send.at[way, 0, c], z_recv.at[way, 1, 0, c], target),
            remote(v_held.at[2 + other, c], v_held.at[first + other, c], pass_send.at[way, 1, c], z_recv.at[way, 1, 1, c], target),
        ]

    def own_in(c):
        return [
            pltpu.make_async_copy(columns(q_ref, side, c), q_held.at[side, c], own_sem.at[0, c]),
            pltpu.make_async_copy(columns(k_ref, side, c), k_held.at[2 + side, c], own_sem.at[1, c]),
            pltpu.make_async_copy(columns(v_ref, side, c), v_held.at[2 + side, c], own_sem.at[2, c]),
        ]

    def back(c):
        return remote(stage.at[c], done.at[side * half + c], back_send.at[c], back_recv.at[c], pair)

    vis_in = pltpu.make_async_copy(vis_ref, vis_held.at[side], vis_sem.at[0])
    vis_out = remote(vis_ref, vis_held.at[side], vis_sem.at[1], vis_sem.at[2], pair)
    vis_got = remote(vis_ref, vis_held.at[1 - side], vis_sem.at[1], vis_sem.at[2], pair)

    barrier = pltpu.get_barrier_semaphore()

    def greet(target):
        pl.semaphore_signal(barrier, inc=1, device_id={"ctx": target}, device_id_type=pl.DeviceIdType.MESH)

    greet(pair)

    @pl.when(has_up)
    def _():
        greet(up)

    @pl.when(has_down)
    def _():
        greet(down)

    vis_in.start()

    @pl.loop(0, half)
    def _(c):
        for copy in own_in(c):
            copy.start()

    pl.semaphore_wait(barrier, 1 + has_up.astype(jnp.int32) + has_down.astype(jnp.int32))

    vis_out.start()

    @pl.loop(0, half)
    def _(c):
        for copy in to_pair(c):
            copy.start()

        @pl.when(has_up)
        def _():
            for copy in own_out(c, 0):
                copy.start()

        @pl.when(has_down)
        def _():
            for copy in own_out(c, 1):
                copy.start()

    @pl.when(jnp.logical_not(has_down))
    def _():
        k_held[0:2] = jnp.zeros((2,) + k_held.shape[1:], k_held.dtype)
        v_held[0:2] = jnp.zeros((2,) + v_held.shape[1:], v_held.dtype)

    @pl.when(jnp.logical_not(has_up))
    def _():
        k_held[4:6] = jnp.zeros((2,) + k_held.shape[1:], k_held.dtype)
        v_held[4:6] = jnp.zeros((2,) + v_held.shape[1:], v_held.dtype)

    def forward(c):
        for copy in from_pair(c):
            copy.wait_recv()

        @pl.when(has_up)
        def _():
            for copy in pass_on(c, 0):
                copy.start()

        @pl.when(has_down)
        def _():
            for copy in pass_on(c, 1):
                copy.start()

    def attend(c, j):
        q = q_held[j, c]
        seen = [vis_held[j, o : o + 1, :] > 0.0 for o in range(SLOTS)]
        scores, peak = [], None
        for o in range(SLOTS):
            s = lax.dot_general(q, k_held[j + o, c], (((1,), (1,)), ((), ())), preferred_element_type=jnp.float32)
            scores.append(s)
            top = s[:, :HD]
            for lane in range(HD, s.shape[1], HD):
                top = jnp.maximum(top, s[:, lane : lane + HD])
            top = jnp.where(seen[o], top, HIDDEN)
            peak = top if peak is None else jnp.maximum(peak, top)
        peak = jnp.max(peak, axis=1, keepdims=True) * scale
        total, mixture = None, None
        for o in range(SLOTS):
            shift = jnp.where(seen[o][:, :1], peak, SHUT)
            p = jnp.exp2(scores[o] * scale - shift)
            for lane in range(0, p.shape[1], HD):
                part = p[:, lane : lane + HD]
                total = part if total is None else total + part
            part = jnp.dot(p.astype(jnp.bfloat16), v_held[j + o, c], preferred_element_type=jnp.float32)
            mixture = part if mixture is None else mixture + part
        total = jnp.sum(total, axis=1, keepdims=True)
        return (mixture / total).astype(jnp.bfloat16)

    vis_in.wait()
    vis_got.wait_recv()
    forward(0)

    @pl.loop(0, half)
    def _(c):
        @pl.when(c + 1 < half)
        def _():
            forward(c + 1)

        for copy in own_in(c):
            copy.wait()

        @pl.when(has_down)
        def _():
            for copy in own_out(c, 0) + pass_on(c, 0):
                copy.wait_recv()

        @pl.when(has_up)
        def _():
            for copy in own_out(c, 1) + pass_on(c, 1):
                copy.wait_recv()

        stage[c] = attend(c, 1 - side)
        back(c).start()
        done[side * half + c] = attend(c, side)

    @pl.loop(0, half)
    def _(c):
        for copy in to_pair(c):
            copy.wait_send()

        @pl.when(has_up)
        def _():
            for copy in own_out(c, 0) + pass_on(c, 0):
                copy.wait_send()

        @pl.when(has_down)
        def _():
            for copy in own_out(c, 1) + pass_on(c, 1):
                copy.wait_send()

        back(c).wait()

    vis_out.wait_send()
    for h in range(2 * half):
        out_ref[0, :, h * HD : (h + 1) * HD] = done[h]


def per_device(queries, key_rows, value_rows, tile_lists, tile_counts, out_weight):
    tok_rows, channels = queries.shape[1], queries.shape[2]
    tiles = lax.axis_size("ctx")
    heads = channels // HD
    half = heads // 2
    tile_here = lax.axis_index("ctx")
    offsets = jnp.arange(SLOTS, dtype=jnp.int32) - REACH
    in_use = jnp.arange(SLOTS, dtype=jnp.int32) < tile_counts[0, 0]
    matches = (tile_lists[0, 0, :, None] == (tile_here + offsets)[None, :]) & in_use[:, None]
    visible = jnp.any(matches, axis=0).astype(jnp.float32)
    visible = jnp.broadcast_to(jnp.pad(visible, (0, 8 - SLOTS))[:, None], (8, HD))
    any_spec = pl.BlockSpec(memory_space=pl.ANY)
    held = pltpu.VMEM((WINDOW, half, tok_rows, HD), jnp.bfloat16)
    dma = pltpu.SemaphoreType.DMA
    pairs = 2 * tok_rows * SLOTS * tok_rows * half
    attention = pl.pallas_call(
        functools.partial(kernel, tiles),
        out_shape=jax.ShapeDtypeStruct(queries.shape, jnp.bfloat16),
        in_specs=[any_spec] * 4,
        out_specs=pl.BlockSpec(memory_space=pltpu.VMEM),
        scratch_shapes=[
            pltpu.VMEM((2, half, tok_rows, HD), jnp.bfloat16),
            held,
            held,
            pltpu.VMEM((2, 8, HD), jnp.float32),
            pltpu.VMEM((heads, tok_rows, HD), jnp.bfloat16),
            pltpu.VMEM((half, tok_rows, HD), jnp.bfloat16),
            dma((3, half)),
            dma((3,)),
            dma((3, half)),
            dma((3, half)),
            dma((2, 2, half)),
            dma((2, 2, half)),
            dma((2, 2, 2, half)),
            dma((half,)),
            dma((half,)),
        ],
        compiler_params=pltpu.CompilerParams(
            collective_id=0, has_side_effects=True, vmem_limit_bytes=44 * 1024 * 1024
        ),
        cost_estimate=pl.CostEstimate(
            flops=4 * pairs * HD, bytes_accessed=60_000_000, transcendentals=pairs
        ),
    )(queries, key_rows, value_rows, visible)
    gathered = lax.all_gather(out_weight, "dp", axis=0, tiled=True)
    projected = jnp.dot(attention[0], gathered, preferred_element_type=jnp.float32)
    return projected.astype(jnp.bfloat16)[None]


def solution(mesh):
    in_specs = (
        P("dp", "ctx", None),
        P("dp", "ctx", None),
        P("dp", "ctx", None),
        P("dp", "ctx", None),
        P("dp", "ctx"),
        P("dp", None),
    )
    out_specs = P("dp", "ctx", None)
    return jax.shard_map(
        per_device, mesh=mesh, in_specs=in_specs, out_specs=out_specs, check_vma=False
    )
```

time: 210 us -> 87.4 us (0.42)
  waiting for transfers between devices: 94.3 us -> 0.73 us
  Pallas kernels: 0 us -> 64.3 us
  matrix products: 46.3 us -> 5.36 us
  local copies, waits for them, and re-layouts: 22.2 us -> 2.62 us
  starting transfers between devices: 13.8 us -> 0.01 us
  other arithmetic: 9.69 us -> 0.11 us
  loops' own time: 7.84 us -> 0 us
    ppermute x4 -> x0, waiting for transfers between devices: 94.3 us -> none  [from_behind(): return lax.ppermute(value, axis, pairs)]
    pallas_call x0 -> x1, Pallas kernels: none -> 64.3 us  [per_device(): pl.pallas_call(functools.partial(kernel, tiles), out_shape=jax.ShapeDtype...]
    dot_general x25 -> x1, matrix products: 46.3 us -> 5.36 us  [per_device(): jnp.dot(attention[0], gathered, preferred_element_type=jnp.float32)]
    ppermute x4 -> x0, starting transfers between devices: 13.8 us -> none  [from_behind(): return lax.ppermute(value, axis, pairs)]
    another operation x1 -> x0, loops' own time: 7.84 us -> none  [masked_video(): per_heads = lax.map(per_head, jnp.arange(HEADS, dtype=jnp.int32))]
    reduce_sum x12 -> x0, other arithmetic: 7.57 us -> none  [per_head(): totals = jnp.sum(exponent, axis=1, keepdims=True)]
    dynamic_slice x12 -> x0, local copies, waits for them, and re-layouts: 7.37 us -> none  [masked_video(): per_heads = lax.map(per_head, jnp.arange(HEADS, dtype=jnp.int32))]
    squeeze x1 -> x0, local copies, waits for them, and re-layouts: 4.72 us -> none  [per_device(): windowed[1, 0]]
  transfers between devices with their start and end apart: 5 -> 1, of which waited for: 3 -> 0; matrix products, arithmetic and copies ran while one was open for 34% -> 0% of each run, Pallas kernels for 0% -> 74%
where the time goes in v1:
time: 87.4 us; the launch traced here: 87.2 us
  Pallas kernels  64.3 us (74%)
  between operations  14.1 us (16%)
  matrix products  5.36 us (6%)
  local copies, waits for them, and re-layouts  2.62 us (3%)
    pallas_call x1, Pallas kernels, per_device(): pl.pallas_call(functools.partial(kernel, tiles), out_shape=jax.ShapeDtype...  64.3 us
    dot_general x1, matrix products, per_device(): jnp.dot(attention[0], gathered, preferred_element_type=jnp.float32)  5.36 us
    unnamed x8, local copies, waits for them, and re-layouts  2.55 us
  transfers between devices with their start and end apart: 1, of which 0 were waited for; matrix products, arithmetic and copies ran while one was open for 0% of the time, Pallas kernels for 74%

profile of v1, /device:TPU:0, one launch (start us, length us, event | category | flops | bytes accessed | tf_op | source)
XLA Modules:
  0.0 87.2 jit_solution(9042320496569852981)
XLA Ops:
  6.5 0.0 copy-start.3
  6.5 0.0 copy-start
  6.5 0.0 all-gather.2.cloned.1.call-start
  6.5 0.7 all-gather.2.cloned.1.call-update
  7.9 0.0 copy-done.3
  7.9 0.1 and_reduce_fusion
  8.0 0.1 broadcast_in_dim.4.vis_ref
  8.1 0.0 copy-done
  8.1 0.0 copy-start.1
  8.1 1.3 %copy-done.1 = bf16[1,384,1536]{2,1,0:T(8,128)(2,1)S(1)} copy-done((bf16[1,384,1536]{2,1,0:T(8,128)(2,1)S(1)}, bf16[1,384,1536]{2,1,0:T(8,128)(2,1)}, u32[]{:S(2)}) %copy-start.1) | copy-done | bytes 1179672
  9.4 0.0 copy-start.2
  9.4 1.3 %copy-done.2 = bf16[1,384,1536]{2,1,0:T(8,128)(2,1)S(1)} copy-done((bf16[1,384,1536]{2,1,0:T(8,128)(2,1)S(1)}, bf16[1,384,1536]{2,1,0:T(8,128)(2,1)}, u32[]{:S(2)}) %copy-start.2) | copy-done | bytes 1179672
  10.7 64.3 %shard_map.64 = bf16[1,384,1536]{2,1,0:T(8,128)(2,1)S(1)} custom-call(bf16[1,384,1536]{2,1,0:T(8,128)(2,1)S(1)} %copy-done, bf16[1,384,1536]{2,1,0:T(8,128)(2,1)S(1)} %copy-done.1, bf16[1,384,1536]{2,1,0:T(8,128)(2,1)S(1)} %copy-done.2, f32[8,128]{1,0:T(8,128)S(1)} %broadcast_in_dim.4.vis_ref), custom_call_target="tpu_custom_call" | custom-call | flops 4529848320 | bytes 60000000 | tf_op jit(solution)/shard_map/pallas_call | solution.py:238
  74.9 0.0 all-gather.2.cloned.1.call-done
  75.0 5.4 %fusion = bf16[1,384,1536]{2,1,0:T(8,128)(2,1)} fusion(bf16[1536,1536]{1,0:T(8,128)(2,1)} %all-gather.2.cloned.1.call-done, bf16[1,384,1536]{2,1,0:T(8,128)(2,1)S(1)} %shard_map.64), kind=kOutput, calls=%fused_computation.1 | convolution fusion | flops 1812529152 | bytes 7077888 | tf_op jit(solution)/shard_map/dot_general | solution.py:268
  (3 shorter events, 0.0 us)
Async XLA Ops:
  6.5 1.4 %copy-start.3 = (s32[1,1,5]{2,1,0:T(1,128)S(1)}, s32[1,1,5]{2,1,0:T(1,128)}, u32[]{:S(2)}) copy-start(s32[1,1,5]{2,1,0:T(1,128)} %param.9) | copy-start | bytes 64
  6.5 1.6 %copy-start = (bf16[1,384,1536]{2,1,0:T(8,128)(2,1)S(1)}, bf16[1,384,1536]{2,1,0:T(8,128)(2,1)}, u32[]{:S(2)}) copy-start(bf16[1,384,1536]{2,1,0:T(8,128)(2,1)} %q_ref.1) | copy-start | bytes 3538948
  6.5 68.4 %all-gather.2.cloned.1.call-start = ((), (), s32[]{:S(2)}) async-start(), calls=%async_computation | async-start | bytes 5898240 | tf_op jit(solution)/shard_map/all_gather | solution.py:267
  8.1 1.3 %copy-start.1 = (bf16[1,384,1536]{2,1,0:T(8,128)(2,1)S(1)}, bf16[1,384,1536]{2,1,0:T(8,128)(2,1)}, u32[]{:S(2)}) copy-start(bf16[1,384,1536]{2,1,0:T(8,128)(2,1)} %k_ref.1) | copy-start | bytes 3538948
  9.4 1.3 %copy-start.2 = (bf16[1,384,1536]{2,1,0:T(8,128)(2,1)S(1)}, bf16[1,384,1536]{2,1,0:T(8,128)(2,1)}, u32[]{:S(2)}) copy-start(bf16[1,384,1536]{2,1,0:T(8,128)(2,1)} %v_ref.1) | copy-start | bytes 3538948
Sparse Core Ops, SparseCore 0:
  8.9 40.1 all-gather.1

commit v2 on v1

--- a/solution.py
+++ b/solution.py
@@ -14,13 +14,18 @@
 WINDOW = 6
 HIDDEN = -1e30
 SHUT = 1e30
-
-
-def kernel(tiles, q_ref, k_ref, v_ref, vis_ref, out_ref,
-           q_held, k_held, v_held, vis_held, done, stage,
-           own_sem, vis_sem, pair_send, pair_recv, own_send, pass_send, z_recv, back_send, back_recv):
+BLOCK = 256
+
+
+def kernel(tiles, shards, q_ref, k_ref, v_ref, vis_ref, w_ref, out_ref,
+           q_held, k_held, v_held, vis_held, done, stage, w_held,
+           w_own, w_send, w_recv, w_pass, w_core, own_sem, vis_sem, pair_send, pair_recv, own_send, pass_send, z_recv, back_send, back_recv):
     half = q_held.shape[1]
     me = lax.axis_index("ctx")
+    row = lax.axis_index("dp")
+    sibling = row + 1 - 2 * lax.rem(row, 2)
+    depth = w_ref.shape[0]
+    chips = shards // 2
     side = lax.rem(me, 2)
     pair = me + 1 - 2 * side
     has_up = me + 2 < tiles
@@ -74,8 +79,32 @@
             pltpu.make_async_copy(columns(v_ref, side, c), v_held.at[2 + side, c], own_sem.at[2, c]),
         ]
 
+    def head(which, c):
+        return done.at[:, pl.ds(pl.multiple_of((which * half + c) * HD, HD), HD)]
+
     def back(c):
-        return remote(stage.at[c], done.at[side * half + c], back_send.at[c], back_recv.at[c], pair)
+        return remote(stage.at[c], head(side, c), back_send.at[c], back_recv.at[c], pair)
+
+    def shard(owner):
+        return w_held.at[pl.ds(pl.multiple_of(owner * depth, depth), depth)]
+
+    def w_copy(src, owner, send, recv, target):
+        return pltpu.make_async_remote_copy(
+            src_ref=src, dst_ref=shard(owner), send_sem=send, recv_sem=recv,
+            device_id={"dp": target}, device_id_type=pl.DeviceIdType.MESH,
+        )
+
+    def w_chip(k):
+        return w_copy(w_ref, row, w_send.at[k], w_recv.at[k], lax.rem(row + 2 * k, shards))
+
+    def w_from(k):
+        return lax.rem(row + shards - 2 * k, shards)
+
+    def w_sibling(k):
+        src = w_ref if k == 0 else shard(w_from(k))
+        return w_copy(src, w_from(k), w_pass.at[k], w_core.at[k], sibling)
+
+    w_in = pltpu.make_async_copy(w_ref, shard(row), w_own.at[0])
 
     vis_in = pltpu.make_async_copy(vis_ref, vis_held.at[side], vis_sem.at[0])
     vis_out = remote(vis_ref, vis_held.at[side], vis_sem.at[1], vis_sem.at[2], pair)
@@ -86,7 +115,13 @@
     def greet(target):
         pl.semaphore_signal(barrier, inc=1, device_id={"ctx": target}, device_id_type=pl.DeviceIdType.MESH)
 
+    def greet_row(target):
+        pl.semaphore_signal(barrier, inc=1, device_id={"dp": target}, device_id_type=pl.DeviceIdType.MESH)
+
     greet(pair)
+    greet_row(sibling)
+    for k in range(1, chips):
+        greet_row(lax.rem(row + 2 * k, shards))
 
     @pl.when(has_up)
     def _():
@@ -103,7 +138,7 @@
         for copy in own_in(c):
             copy.start()
 
-    pl.semaphore_wait(barrier, 1 + has_up.astype(jnp.int32) + has_down.astype(jnp.int32))
+    pl.semaphore_wait(barrier, 1 + chips + has_up.astype(jnp.int32) + has_down.astype(jnp.int32))
 
     vis_out.start()
 
@@ -121,6 +156,11 @@
         def _():
             for copy in own_out(c, 1):
                 copy.start()
+
+    w_in.start()
+    for k in range(1, chips):
+        w_chip(k).start()
+    w_sibling(0).start()
 
     @pl.when(jnp.logical_not(has_down))
     def _():
@@ -196,7 +236,13 @@
 
         stage[c] = attend(c, 1 - side)
         back(c).start()
-        done[side * half + c] = attend(c, side)
+        head(side, c)[...] = attend(c, side)
+
+        @pl.when(c == half // 2)
+        def _():
+            for k in range(1, chips):
+                w_chip(k).wait_recv()
+                w_sibling(k).start()
 
     @pl.loop(0, half)
     def _(c):
@@ -216,8 +262,17 @@
         back(c).wait()
 
     vis_out.wait_send()
-    for h in range(2 * half):
-        out_ref[0, :, h * HD : (h + 1) * HD] = done[h]
+    w_in.wait()
+    for k in range(1, chips):
+        w_chip(k).wait_send()
+    for k in range(chips):
+        w_sibling(k).wait()
+
+    @pl.loop(0, out_ref.shape[2] // BLOCK)
+    def _(n):
+        cols = pl.ds(pl.multiple_of(n * BLOCK, BLOCK), BLOCK)
+        product = jnp.dot(done[...], w_held[:, cols], preferred_element_type=jnp.float32)
+        out_ref[0, :, cols] = product.astype(jnp.bfloat16)
 
 
 def per_device(queries, key_rows, value_rows, tile_lists, tile_counts, out_weight):
@@ -235,18 +290,26 @@
     held = pltpu.VMEM((WINDOW, half, tok_rows, HD), jnp.bfloat16)
     dma = pltpu.SemaphoreType.DMA
     pairs = 2 * tok_rows * SLOTS * tok_rows * half
-    attention = pl.pallas_call(
-        functools.partial(kernel, tiles),
-        out_shape=jax.ShapeDtypeStruct(queries.shape, jnp.bfloat16),
-        in_specs=[any_spec] * 4,
+    shards = lax.axis_size("dp")
+    chips = shards // 2
+    return pl.pallas_call(
+        functools.partial(kernel, tiles, shards),
+        out_shape=jax.ShapeDtypeStruct((1, tok_rows, out_weight.shape[1]), jnp.bfloat16),
+        in_specs=[any_spec] * 5,
         out_specs=pl.BlockSpec(memory_space=pltpu.VMEM),
         scratch_shapes=[
             pltpu.VMEM((2, half, tok_rows, HD), jnp.bfloat16),
             held,
             held,
             pltpu.VMEM((2, 8, HD), jnp.float32),
-            pltpu.VMEM((heads, tok_rows, HD), jnp.bfloat16),
+            pltpu.VMEM((tok_rows, channels), jnp.bfloat16),
             pltpu.VMEM((half, tok_rows, HD), jnp.bfloat16),
+            pltpu.VMEM((channels, out_weight.shape[1]), jnp.bfloat16),
+            dma((1,)),
+            dma((chips,)),
+            dma((chips,)),
+            dma((chips,)),
+            dma((chips,)),
             dma((3, half)),
             dma((3,)),
             dma((3, half)),
@@ -258,15 +321,12 @@
             dma((half,)),
         ],
         compiler_params=pltpu.CompilerParams(
-            collective_id=0, has_side_effects=True, vmem_limit_bytes=44 * 1024 * 1024
+            collective_id=0, has_side_effects=True, vmem_limit_bytes=60 * 1024 * 1024
         ),
         cost_estimate=pl.CostEstimate(
             flops=4 * pairs * HD, bytes_accessed=60_000_000, transcendentals=pairs
         ),
-    )(queries, key_rows, value_rows, visible)
-    gathered = lax.all_gather(out_weight, "dp", axis=0, tiled=True)
-    projected = jnp.dot(attention[0], gathered, preferred_element_type=jnp.float32)
-    return projected.astype(jnp.bfloat16)[None]
+    )(queries, key_rows, value_rows, visible, out_weight)
 
 
 def solution(mesh):

time: 87.4 us -> 74.2 us (0.85)
  between operations: 14.1 us -> 0.68 us
  matrix products: 5.36 us -> 0 us
  Pallas kernels: 64.3 us -> 69.6 us
    dot_general x1 -> x0, matrix products: 5.36 us -> none  [per_device(): jnp.dot(attention[0], gathered, preferred_element_type=jnp.float32)]
    pallas_call x1, Pallas kernels: 64.3 us -> 69.6 us  [per_device(): pl.pallas_call(functools.partial(kernel, tiles, shards), out_shape=jax.Sh...]
    unnamed x8 -> x1, local copies, waits for them, and re-layouts: 2.55 us -> 2.36 us
  transfers between devices with their start and end apart: 1 -> 0, of which waited for: 0 -> 0; matrix products, arithmetic and copies ran while one was open for 0% -> 0% of each run, Pallas kernels for 74% -> 0%
where the time goes in v2:
time: 74.2 us; the launch traced here: 74.1 us
  Pallas kernels  69.6 us (94%)
  local copies, waits for them, and re-layouts  3.02 us (4%)
  other arithmetic  0.76 us (1%)
    pallas_call x1, Pallas kernels, per_device(): pl.pallas_call(functools.partial(kernel, tiles, shards), out_shape=jax.Sh...  69.6 us
    unnamed x1, local copies, waits for them, and re-layouts  2.36 us

profile of v2, /device:TPU:0, one launch (start us, length us, event | category | flops | bytes accessed | tf_op | source)
XLA Modules:
  0.0 74.1 jit_solution(11148527529987964415)
XLA Ops:
  0.7 0.7 %and_reduce_fusion = pred[5]{0:T(512)(128)(4,1)S(1)} fusion(s32[5]{0:T(128)S(1)} %add_add_fusion, s32[5]{0:T(128)} %bitcast.3, pred[5]{0:T(512)(128)(4,1)S(1)} %iota_compare_fusion), kind=kLoop, calls=%fused_computation | loop fusion | flops 70 | bytes 50 | tf_op jit(solution)/shard_map/reduce_or | solution.py:287
  1.4 0.7 broadcast_in_dim.2.vis_ref
  2.1 69.6 %shard_map.64 = bf16[1,384,1536]{2,1,0:T(8,128)(2,1)} custom-call(bf16[1,384,1536]{2,1,0:T(8,128)(2,1)} %q_ref.1, bf16[1,384,1536]{2,1,0:T(8,128)(2,1)} %k_ref.1, bf16[1,384,1536]{2,1,0:T(8,128)(2,1)} %v_ref.1, f32[8,128]{1,0:T(8,128)} %broadcast_in_dim.2.vis_ref, bf16[384,1536]{1,0:T(8,128)(2,1)} %w_ref.1), custom_call_target="tpu_custom_call" | custom-call | flops 4529848320 | bytes 60000000 | tf_op jit(solution)/shard_map/pallas_call | solution.py:295
  71.7 2.4 %copy.9 = bf16[1,384,1536]{2,1,0:T(8,128)(2,1)} copy(bf16[1,384,1536]{2,1,0:T(8,128)(2,1)} %shard_map.64) | data formatting | bytes 2359296
  (3 shorter events, 0.0 us)

commit v3 on v2

--- a/solution.py
+++ b/solution.py
@@ -17,8 +17,8 @@
 BLOCK = 256
 
 
-def kernel(tiles, shards, q_ref, k_ref, v_ref, vis_ref, w_ref, out_ref,
-           q_held, k_held, v_held, vis_held, done, stage, w_held,
+def kernel(tiles, shards, q_ref, k_ref, v_ref, lists_ref, counts_ref, w_ref, out_ref,
+           lists_held, counts_held, vis_mine, q_held, k_held, v_held, vis_held, done, stage, w_held,
            w_own, w_send, w_recv, w_pass, w_core, own_sem, vis_sem, pair_send, pair_recv, own_send, pass_send, z_recv, back_send, back_recv):
     half = q_held.shape[1]
     me = lax.axis_index("ctx")
@@ -106,9 +106,10 @@
 
     w_in = pltpu.make_async_copy(w_ref, shard(row), w_own.at[0])
 
-    vis_in = pltpu.make_async_copy(vis_ref, vis_held.at[side], vis_sem.at[0])
-    vis_out = remote(vis_ref, vis_held.at[side], vis_sem.at[1], vis_sem.at[2], pair)
-    vis_got = remote(vis_ref, vis_held.at[1 - side], vis_sem.at[1], vis_sem.at[2], pair)
+    lists_in = pltpu.make_async_copy(lists_ref, lists_held, vis_sem.at[0])
+    counts_in = pltpu.make_async_copy(counts_ref, counts_held, vis_sem.at[3])
+    vis_out = remote(vis_mine, vis_held.at[side], vis_sem.at[1], vis_sem.at[2], pair)
+    vis_got = remote(vis_mine, vis_held.at[1 - side], vis_sem.at[1], vis_sem.at[2], pair)
 
     barrier = pltpu.get_barrier_semaphore()
 
@@ -131,7 +132,8 @@
     def _():
         greet(down)
 
-    vis_in.start()
+    lists_in.start()
+    counts_in.start()
 
     @pl.loop(0, half)
     def _(c):
@@ -140,11 +142,9 @@
 
     pl.semaphore_wait(barrier, 1 + chips + has_up.astype(jnp.int32) + has_down.astype(jnp.int32))
 
-    vis_out.start()
-
-    @pl.loop(0, half)
-    def _(c):
-        for copy in to_pair(c):
+    @pl.loop(0, half)
+    def _(c):
+        for copy in to_pair(c)[:2]:
             copy.start()
 
         @pl.when(has_up)
@@ -162,6 +162,17 @@
         w_chip(k).start()
     w_sibling(0).start()
 
+    lists_in.wait()
+    counts_in.wait()
+    listed = lists_held[0]
+    live = lax.broadcasted_iota(jnp.int32, listed.shape, 1) < counts_held[...]
+    for o in range(SLOTS):
+        match = jnp.where((listed == me + (o - REACH)) & live, 1.0, 0.0)
+        row_seen = jnp.max(match, axis=1, keepdims=True)
+        vis_mine[o : o + 1, :] = jnp.broadcast_to(row_seen, (1, HD))
+        vis_held[side, o : o + 1, :] = jnp.broadcast_to(row_seen, (1, HD))
+    vis_out.start()
+
     @pl.when(jnp.logical_not(has_down))
     def _():
         k_held[0:2] = jnp.zeros((2,) + k_held.shape[1:], k_held.dtype)
@@ -172,9 +183,11 @@
         k_held[4:6] = jnp.zeros((2,) + k_held.shape[1:], k_held.dtype)
         v_held[4:6] = jnp.zeros((2,) + v_held.shape[1:], v_held.dtype)
 
-    def forward(c):
-        for copy in from_pair(c):
+    @pl.loop(0, half)
+    def _(c):
+        for copy in from_pair(c)[:2]:
             copy.wait_recv()
+        to_pair(c)[2].start()
 
         @pl.when(has_up)
         def _():
@@ -211,18 +224,13 @@
         total = jnp.sum(total, axis=1, keepdims=True)
         return (mixture / total).astype(jnp.bfloat16)
 
-    vis_in.wait()
     vis_got.wait_recv()
-    forward(0)
-
-    @pl.loop(0, half)
-    def _(c):
-        @pl.when(c + 1 < half)
-        def _():
-            forward(c + 1)
-
+
+    @pl.loop(0, half)
+    def _(c):
         for copy in own_in(c):
             copy.wait()
+        from_pair(c)[2].wait_recv()
 
         @pl.when(has_down)
         def _():
@@ -280,13 +288,7 @@
     tiles = lax.axis_size("ctx")
     heads = channels // HD
     half = heads // 2
-    tile_here = lax.axis_index("ctx")
-    offsets = jnp.arange(SLOTS, dtype=jnp.int32) - REACH
-    in_use = jnp.arange(SLOTS, dtype=jnp.int32) < tile_counts[0, 0]
-    matches = (tile_lists[0, 0, :, None] == (tile_here + offsets)[None, :]) & in_use[:, None]
-    visible = jnp.any(matches, axis=0).astype(jnp.float32)
-    visible = jnp.broadcast_to(jnp.pad(visible, (0, 8 - SLOTS))[:, None], (8, HD))
-    any_spec = pl.BlockSpec(memory_space=pl.ANY)
+    hbm_spec = pl.BlockSpec(memory_space=pltpu.HBM)
     held = pltpu.VMEM((WINDOW, half, tok_rows, HD), jnp.bfloat16)
     dma = pltpu.SemaphoreType.DMA
     pairs = 2 * tok_rows * SLOTS * tok_rows * half
@@ -294,10 +296,13 @@
     chips = shards // 2
     return pl.pallas_call(
         functools.partial(kernel, tiles, shards),
-        out_shape=jax.ShapeDtypeStruct((1, tok_rows, out_weight.shape[1]), jnp.bfloat16),
-        in_specs=[any_spec] * 5,
+        out_shape=pltpu.VMEM((1, tok_rows, out_weight.shape[1]), jnp.bfloat16),
+        in_specs=[hbm_spec] * 6,
         out_specs=pl.BlockSpec(memory_space=pltpu.VMEM),
         scratch_shapes=[
+            pltpu.VMEM(tile_lists.shape, jnp.int32),
+            pltpu.VMEM(tile_counts.shape, jnp.int32),
+            pltpu.VMEM((8, HD), jnp.float32),
             pltpu.VMEM((2, half, tok_rows, HD), jnp.bfloat16),
             held,
             held,
@@ -311,7 +316,7 @@
             dma((chips,)),
             dma((chips,)),
             dma((3, half)),
-            dma((3,)),
+            dma((4,)),
             dma((3, half)),
             dma((3, half)),
             dma((2, 2, half)),
@@ -326,7 +331,7 @@
         cost_estimate=pl.CostEstimate(
             flops=4 * pairs * HD, bytes_accessed=60_000_000, transcendentals=pairs
         ),
-    )(queries, key_rows, value_rows, visible, out_weight)
+    )(queries, key_rows, value_rows, tile_lists, tile_counts, out_weight)
 
 
 def solution(mesh):

time: 74.2 us -> 68.1 us (0.918)
  Pallas kernels: 69.6 us -> 66.3 us
  local copies, waits for them, and re-layouts: 3.02 us -> 1.02 us
  other arithmetic: 0.76 us -> 0 us
    pallas_call x1, Pallas kernels: 69.6 us -> 66.3 us  [per_device(): pl.pallas_call(functools.partial(kernel, tiles, shards), out_shape=pltpu....]
    unnamed x1, local copies, waits for them, and re-layouts: 2.36 us -> 1.02 us
    reduce_or x1 -> x0, other arithmetic: 0.75 us -> none  [per_device(): visible = jnp.any(matches, axis=0).astype(jnp.float32)]
where the time goes in v3:
time: 68.1 us; the launch traced here: 67.9 us
  Pallas kernels  66.3 us (97%)
  local copies, waits for them, and re-layouts  1.02 us (1%)
    pallas_call x1, Pallas kernels, per_device(): pl.pallas_call(functools.partial(kernel, tiles, shards), out_shape=pltpu....  66.3 us

profile of v3, /device:TPU:0, one launch (start us, length us, event | category | flops | bytes accessed | tf_op | source)
XLA Modules:
  0.0 67.9 jit_solution(4581617748238976461)
XLA Ops:
  0.7 66.3 %shard_map.64 = bf16[1,384,1536]{2,1,0:T(8,128)(2,1)S(1)} custom-call(bf16[1,384,1536]{2,1,0:T(8,128)(2,1)} %q_ref.1, bf16[1,384,1536]{2,1,0:T(8,128)(2,1)} %k_ref.1, bf16[1,384,1536]{2,1,0:T(8,128)(2,1)} %v_ref.1, s32[1,1,5]{2,1,0:T(1,128)} %lists_ref.1, s32[1,1]{1,0:T(1,128)S(6)} %copy.9.counts_ref, bf16[384,1536]{1,0:T(8,128)(2,1)} %w_ref.1), custom_call_target="tpu_custom_call" | custom-call | flops 4529848320 | bytes 60000000 | tf_op jit(solution)/shard_map/pallas_call | solution.py:297
  66.9 1.0 %copy.8 = bf16[1,384,1536]{2,1,0:T(8,128)(2,1)} copy(bf16[1,384,1536]{2,1,0:T(8,128)(2,1)S(1)} %shard_map.64) | data formatting | bytes 2359296

commit v4 on v3

--- a/solution.py
+++ b/solution.py
@@ -18,7 +18,7 @@
 
 
 def kernel(tiles, shards, q_ref, k_ref, v_ref, lists_ref, counts_ref, w_ref, out_ref,
-           lists_held, counts_held, vis_mine, q_held, k_held, v_held, vis_held, done, stage, w_held,
+           lists_held, counts_held, vis_mine, q_held, k_held, v_held, vis_held, done, stage, w_held, peak_kept, total_kept, mixture_kept, partial,
            w_own, w_send, w_recv, w_pass, w_core, own_sem, vis_sem, pair_send, pair_recv, own_send, pass_send, z_recv, back_send, back_recv):
     half = q_held.shape[1]
     me = lax.axis_index("ctx")
@@ -183,6 +183,51 @@
         k_held[4:6] = jnp.zeros((2,) + k_held.shape[1:], k_held.dtype)
         v_held[4:6] = jnp.zeros((2,) + v_held.shape[1:], v_held.dtype)
 
+    def attend(c, j, offsets, first):
+        q = q_held[j, c]
+        seen = [vis_held[j, pl.ds(o, 1), :] > 0.0 for o in offsets]
+        scores, peak = [], None
+        for o, see in zip(offsets, seen):
+            s = lax.dot_general(q, k_held[j + o, c], (((1,), (1,)), ((), ())), preferred_element_type=jnp.float32)
+            scores.append(s)
+            top = s[:, :HD]
+            for lane in range(HD, s.shape[1], HD):
+                top = jnp.maximum(top, s[:, lane : lane + HD])
+            top = jnp.where(see, top, HIDDEN)
+            peak = top if peak is None else jnp.maximum(peak, top)
+        peak = jnp.max(peak, axis=1, keepdims=True) * scale
+        if first:
+            total, mixture = None, None
+        else:
+            before = peak_kept[j, c][:, :1]
+            peak = jnp.maximum(peak, before)
+            fade = jnp.exp2(before - peak)
+            total, mixture = total_kept[j, c] * fade, mixture_kept[j, c] * fade
+        for o, see, s in zip(offsets, seen, scores):
+            shift = jnp.where(see[:, :1], peak, SHUT)
+            p = jnp.exp2(s * scale - shift)
+            for lane in range(0, p.shape[1], HD):
+                part = p[:, lane : lane + HD]
+                total = part if total is None else total + part
+            part = jnp.dot(p.astype(jnp.bfloat16), v_held[j + o, c], preferred_element_type=jnp.float32)
+            mixture = part if mixture is None else mixture + part
+        if first:
+            peak_kept[j, c] = jnp.broadcast_to(peak, mixture.shape)
+            total_kept[j, c] = total
+            mixture_kept[j, c] = mixture
+            return None
+        total = jnp.sum(total, axis=1, keepdims=True)
+        return (mixture / total).astype(jnp.bfloat16)
+
+    early = (half - 2) * HD
+    spans = [(0, early), (half * HD, half * HD + early)]
+    rest = [(early, half * HD), (half * HD + early, 2 * half * HD)]
+
+    def project(pieces, cols):
+        return sum(
+            jnp.dot(done[:, a:b], w_held[a:b, cols], preferred_element_type=jnp.float32) for a, b in pieces
+        )
+
     @pl.loop(0, half)
     def _(c):
         for copy in from_pair(c)[:2]:
@@ -199,58 +244,68 @@
             for copy in pass_on(c, 1):
                 copy.start()
 
-    def attend(c, j):
-        q = q_held[j, c]
-        seen = [vis_held[j, o : o + 1, :] > 0.0 for o in range(SLOTS)]
-        scores, peak = [], None
-        for o in range(SLOTS):
-            s = lax.dot_general(q, k_held[j + o, c], (((1,), (1,)), ((), ())), preferred_element_type=jnp.float32)
-            scores.append(s)
-            top = s[:, :HD]
-            for lane in range(HD, s.shape[1], HD):
-                top = jnp.maximum(top, s[:, lane : lane + HD])
-            top = jnp.where(seen[o], top, HIDDEN)
-            peak = top if peak is None else jnp.maximum(peak, top)
-        peak = jnp.max(peak, axis=1, keepdims=True) * scale
-        total, mixture = None, None
-        for o in range(SLOTS):
-            shift = jnp.where(seen[o][:, :1], peak, SHUT)
-            p = jnp.exp2(scores[o] * scale - shift)
-            for lane in range(0, p.shape[1], HD):
-                part = p[:, lane : lane + HD]
-                total = part if total is None else total + part
-            part = jnp.dot(p.astype(jnp.bfloat16), v_held[j + o, c], preferred_element_type=jnp.float32)
-            mixture = part if mixture is None else mixture + part
-        total = jnp.sum(total, axis=1, keepdims=True)
-        return (mixture / total).astype(jnp.bfloat16)
+        for copy in own_in(c):
+            copy.wait()
+
+        @pl.when(has_down)
+        def _():
+            for copy in own_out(c, 0):
+                copy.wait_recv()
+
+        @pl.when(has_up)
+        def _():
+            for copy in own_out(c, 1):
+                copy.wait_recv()
+
+        attend(c, side, [0, 2 - side, 3 - side, 4], True)
 
     vis_got.wait_recv()
 
     @pl.loop(0, half)
     def _(c):
-        for copy in own_in(c):
-            copy.wait()
         from_pair(c)[2].wait_recv()
-
-        @pl.when(has_down)
-        def _():
-            for copy in own_out(c, 0) + pass_on(c, 0):
-                copy.wait_recv()
-
-        @pl.when(has_up)
-        def _():
-            for copy in own_out(c, 1) + pass_on(c, 1):
-                copy.wait_recv()
-
-        stage[c] = attend(c, 1 - side)
-        back(c).start()
-        head(side, c)[...] = attend(c, side)
-
-        @pl.when(c == half // 2)
+        attend(c, 1 - side, [1, 2, 3], True)
+
+        @pl.when(c == 1)
         def _():
             for k in range(1, chips):
                 w_chip(k).wait_recv()
                 w_sibling(k).start()
+
+        @pl.when(c == half - 1)
+        def _():
+            w_in.wait()
+            for k in range(chips):
+                w_sibling(k).wait()
+            for e in range(half - 2):
+                back(e).wait_recv()
+
+            @pl.loop(0, out_ref.shape[2] // BLOCK)
+            def _(n):
+                cols = pl.ds(pl.multiple_of(n * BLOCK, BLOCK), BLOCK)
+                partial[:, cols] = project(spans, cols)
+
+        @pl.when(has_down)
+        def _():
+            for copy in pass_on(c, 0):
+                copy.wait_recv()
+
+        @pl.when(has_up)
+        def _():
+            for copy in pass_on(c, 1):
+                copy.wait_recv()
+
+        stage[c] = attend(c, 1 - side, [0, 4], False)
+        back(c).start()
+        head(side, c)[...] = attend(c, side, [1 + 2 * side], False)
+
+    for e in range(half - 2, half):
+        back(e).wait_recv()
+
+    @pl.loop(0, out_ref.shape[2] // BLOCK)
+    def _(n):
+        cols = pl.ds(pl.multiple_of(n * BLOCK, BLOCK), BLOCK)
+        out_ref[0, :, cols] = (partial[:, cols] + project(rest, cols)).astype(jnp.bfloat16)
 
     @pl.loop(0, half)
     def _(c):
@@ -267,20 +322,11 @@
             for copy in own_out(c, 1) + pass_on(c, 1):
                 copy.wait_send()
 
-        back(c).wait()
-
-    vis_out.wait_send()
-    w_in.wait()
+        back(c).wait_send()
+
     for k in range(1, chips):
         w_chip(k).wait_send()
-    for k in range(chips):
-        w_sibling(k).wait()
-
-    @pl.loop(0, out_ref.shape[2] // BLOCK)
-    def _(n):
-        cols = pl.ds(pl.multiple_of(n * BLOCK, BLOCK), BLOCK)
-        product = jnp.dot(done[...], w_held[:, cols], preferred_element_type=jnp.float32)
-        out_ref[0, :, cols] = product.astype(jnp.bfloat16)
+    vis_out.wait_send()
 
 
 def per_device(queries, key_rows, value_rows, tile_lists, tile_counts, out_weight):
@@ -290,6 +336,7 @@
     half = heads // 2
     hbm_spec = pl.BlockSpec(memory_space=pltpu.HBM)
     held = pltpu.VMEM((WINDOW, half, tok_rows, HD), jnp.bfloat16)
+    kept = pltpu.VMEM((2, half, tok_rows, HD), jnp.float32)
     dma = pltpu.SemaphoreType.DMA
     pairs = 2 * tok_rows * SLOTS * tok_rows * half
     shards = lax.axis_size("dp")
@@ -310,6 +357,10 @@
             pltpu.VMEM((tok_rows, channels), jnp.bfloat16),
             pltpu.VMEM((half, tok_rows, HD), jnp.bfloat16),
             pltpu.VMEM((channels, out_weight.shape[1]), jnp.bfloat16),
+            kept,
+            kept,
+            kept,
+            pltpu.VMEM((tok_rows, out_weight.shape[1]), jnp.float32),
             dma((1,)),
             dma((chips,)),
             dma((chips,)),

time: 68.1 us -> 67.9 us (level)
  no operation moved by 1% of the time
where the time goes in v4:
time: 67.9 us; the launch traced here: 67.7 us
  Pallas kernels  66.1 us (97%)
  local copies, waits for them, and re-layouts  1.02 us (2%)
    pallas_call x1, Pallas kernels, per_device(): pl.pallas_call(functools.partial(kernel, tiles, shards), out_shape=pltpu....  66.1 us

profile of v4, /device:TPU:0, one launch (start us, length us, event | category | flops | bytes accessed | tf_op | source)
XLA Modules:
  0.0 67.7 jit_solution(6843994162960489084)
XLA Ops:
  0.7 66.1 %shard_map.64 = bf16[1,384,1536]{2,1,0:T(8,128)(2,1)S(1)} custom-call(bf16[1,384,1536]{2,1,0:T(8,128)(2,1)} %q_ref.1, bf16[1,384,1536]{2,1,0:T(8,128)(2,1)} %k_ref.1, bf16[1,384,1536]{2,1,0:T(8,128)(2,1)} %v_ref.1, s32[1,1,5]{2,1,0:T(1,128)} %lists_ref.1, s32[1,1]{1,0:T(1,128)S(6)} %copy.9.counts_ref, bf16[384,1536]{1,0:T(8,128)(2,1)} %w_ref.1), custom_call_target="tpu_custom_call" | custom-call | flops 4529848320 | bytes 60000000 | tf_op jit(solution)/shard_map/pallas_call | solution.py:344
  66.7 1.0 %copy.8 = bf16[1,384,1536]{2,1,0:T(8,128)(2,1)} copy(bf16[1,384,1536]{2,1,0:T(8,128)(2,1)S(1)} %shard_map.64) | data formatting | bytes 2359296

commit v5 on v4

--- a/solution.py
+++ b/solution.py
@@ -15,6 +15,7 @@
 HIDDEN = -1e30
 SHUT = 1e30
 BLOCK = 256
+PIECES = 3
 
 
 def kernel(tiles, shards, q_ref, k_ref, v_ref, lists_ref, counts_ref, w_ref, out_ref,
@@ -60,8 +61,8 @@
     def own_out(c, way):
         first, target = ((0, up), (4, down))[way]
         return [
-            remote(columns(k_ref, side, c), k_held.at[first + side, c], own_send.at[way, 0, c], z_recv.at[way, 0, 0, c], target),
-            remote(columns(v_ref, side, c), v_held.at[first + side, c], own_send.at[way, 1, c], z_recv.at[way, 0, 1, c], target),
+            remote(k_held.at[2 + side, c], k_held.at[first + side, c], own_send.at[way, 0, c], z_recv.at[way, 0, 0, c], target),
+            remote(v_held.at[2 + side, c], v_held.at[first + side, c], own_send.at[way, 1, c], z_recv.at[way, 0, 1, c], target),
         ]
 
     def pass_on(c, way):
@@ -85,26 +86,31 @@
     def back(c):
         return remote(stage.at[c], head(side, c), back_send.at[c], back_recv.at[c], pair)
 
-    def shard(owner):
-        return w_held.at[pl.ds(pl.multiple_of(owner * depth, depth), depth)]
-
-    def w_copy(src, owner, send, recv, target):
+    slab = depth // PIECES
+
+    def shard(owner, i):
+        return w_held.at[pl.ds(pl.multiple_of(owner * depth + i * slab, slab), slab)]
+
+    def mine(i):
+        return w_ref.at[pl.ds(pl.multiple_of(i * slab, slab), slab)]
+
+    def w_copy(src, owner, i, send, recv, target):
         return pltpu.make_async_remote_copy(
-            src_ref=src, dst_ref=shard(owner), send_sem=send, recv_sem=recv,
+            src_ref=src, dst_ref=shard(owner, i), send_sem=send, recv_sem=recv,
             device_id={"dp": target}, device_id_type=pl.DeviceIdType.MESH,
         )
 
-    def w_chip(k):
-        return w_copy(w_ref, row, w_send.at[k], w_recv.at[k], lax.rem(row + 2 * k, shards))
+    def w_chip(k, i):
+        return w_copy(mine(i), row, i, w_send.at[k, i], w_recv.at[k, i], lax.rem(row + 2 * k, shards))
 
     def w_from(k):
         return lax.rem(row + shards - 2 * k, shards)
 
-    def w_sibling(k):
-        src = w_ref if k == 0 else shard(w_from(k))
-        return w_copy(src, w_from(k), w_pass.at[k], w_core.at[k], sibling)
-
-    w_in = pltpu.make_async_copy(w_ref, shard(row), w_own.at[0])
+    def w_sibling(k, i):
+        src = mine(i) if k == 0 else shard(w_from(k), i)
+        return w_copy(src, w_from(k), i, w_pass.at[k, i], w_core.at[k, i], sibling)
+
+    w_in = pltpu.make_async_copy(w_ref, w_held.at[pl.ds(pl.multiple_of(row * depth, depth), depth)], w_own.at[0])
 
     lists_in = pltpu.make_async_copy(lists_ref, lists_held, vis_sem.at[0])
     counts_in = pltpu.make_async_copy(counts_ref, counts_held, vis_sem.at[3])
@@ -146,6 +152,8 @@
     def _(c):
         for copy in to_pair(c)[:2]:
             copy.start()
+        for copy in own_in(c)[1:]:
+            copy.wait()
 
         @pl.when(has_up)
         def _():
@@ -158,9 +166,6 @@
                 copy.start()
 
     w_in.start()
-    for k in range(1, chips):
-        w_chip(k).start()
-    w_sibling(0).start()
 
     lists_in.wait()
     counts_in.wait()
@@ -244,8 +249,13 @@
             for copy in pass_on(c, 1):
                 copy.start()
 
-        for copy in own_in(c):
-            copy.wait()
+        @pl.when(c < PIECES)
+        def _():
+            for k in range(1, chips):
+                w_chip(k, c).start()
+            w_sibling(0, c).start()
+
+        own_in(c)[0].wait()
 
         @pl.when(has_down)
         def _():
@@ -266,17 +276,18 @@
         from_pair(c)[2].wait_recv()
         attend(c, 1 - side, [1, 2, 3], True)
 
-        @pl.when(c == 1)
+        @pl.when(c < PIECES)
         def _():
             for k in range(1, chips):
-                w_chip(k).wait_recv()
-                w_sibling(k).start()
+                w_chip(k, c).wait_recv()
+                w_sibling(k, c).start()
 
         @pl.when(c == half - 1)
         def _():
             w_in.wait()
             for k in range(chips):
-                w_sibling(k).wait()
+                for i in range(PIECES):
+                    w_sibling(k, i).wait()
             for e in range(half - 2):
                 back(e).wait_recv()
 
@@ -325,7 +336,8 @@
         back(c).wait_send()
 
     for k in range(1, chips):
-        w_chip(k).wait_send()
+        for i in range(PIECES):
+            w_chip(k, i).wait_send()
     vis_out.wait_send()
 
 
@@ -362,10 +374,10 @@
             kept,
             pltpu.VMEM((tok_rows, out_weight.shape[1]), jnp.float32),
             dma((1,)),
-            dma((chips,)),
-            dma((chips,)),
-            dma((chips,)),
-            dma((chips,)),
+            dma((chips, PIECES)),
+            dma((chips, PIECES)),
+            dma((chips, PIECES)),
+            dma((chips, PIECES)),
             dma((3, half)),
             dma((4,)),
             dma((3, half)),

time: 67.9 us -> 67.8 us (level)
  no operation moved by 1% of the time
where the time goes in v5:
time: 67.8 us; the launch traced here: 67.6 us
  Pallas kernels  66 us (97%)
  local copies, waits for them, and re-layouts  1.02 us (2%)
    pallas_call x1, Pallas kernels, per_device(): pl.pallas_call(functools.partial(kernel, tiles, shards), out_shape=pltpu....  66 us

profile of v5, /device:TPU:0, one launch (start us, length us, event | category | flops | bytes accessed | tf_op | source)
XLA Modules:
  0.0 67.6 jit_solution(2844340041545392718)
XLA Ops:
  0.7 66.0 %shard_map.64 = bf16[1,384,1536]{2,1,0:T(8,128)(2,1)S(1)} custom-call(bf16[1,384,1536]{2,1,0:T(8,128)(2,1)} %q_ref.1, bf16[1,384,1536]{2,1,0:T(8,128)(2,1)} %k_ref.1, bf16[1,384,1536]{2,1,0:T(8,128)(2,1)} %v_ref.1, s32[1,1,5]{2,1,0:T(1,128)} %lists_ref.1, s32[1,1]{1,0:T(1,128)S(6)} %copy.9.counts_ref, bf16[384,1536]{1,0:T(8,128)(2,1)} %w_ref.1), custom_call_target="tpu_custom_call" | custom-call | flops 4529848320 | bytes 60000000 | tf_op jit(solution)/shard_map/pallas_call | solution.py:356
  66.6 1.0 %copy.8 = bf16[1,384,1536]{2,1,0:T(8,128)(2,1)} copy(bf16[1,384,1536]{2,1,0:T(8,128)(2,1)S(1)} %shard_map.64) | data formatting | bytes 2359296

commit v6 on v5

--- a/solution.py
+++ b/solution.py
@@ -16,6 +16,7 @@
 SHUT = 1e30
 BLOCK = 256
 PIECES = 3
+PARTS = 2
 
 
 def kernel(tiles, shards, q_ref, k_ref, v_ref, lists_ref, counts_ref, w_ref, out_ref,
@@ -83,8 +84,14 @@
     def head(which, c):
         return done.at[:, pl.ds(pl.multiple_of((which * half + c) * HD, HD), HD)]
 
-    def back(c):
-        return remote(stage.at[c], head(side, c), back_send.at[c], back_recv.at[c], pair)
+    part_rows = stage.shape[1] // PARTS
+
+    def back(c, r):
+        rows = slice(r * part_rows, (r + 1) * part_rows)
+        return remote(
+            stage.at[c, rows], done.at[rows, pl.ds(pl.multiple_of((side * half + c) * HD, HD), HD)],
+            back_send.at[c, r], back_recv.at[c, r], pair,
+        )
 
     slab = depth // PIECES
 
@@ -188,8 +195,8 @@
         k_held[4:6] = jnp.zeros((2,) + k_held.shape[1:], k_held.dtype)
         v_held[4:6] = jnp.zeros((2,) + v_held.shape[1:], v_held.dtype)
 
-    def attend(c, j, offsets, first):
-        q = q_held[j, c]
+    def attend(c, j, offsets, first, rows=slice(None), ready=None):
+        q = q_held[j, c, rows]
         seen = [vis_held[j, pl.ds(o, 1), :] > 0.0 for o in offsets]
         scores, peak = [], None
         for o, see in zip(offsets, seen):
@@ -204,10 +211,12 @@
         if first:
             total, mixture = None, None
         else:
-            before = peak_kept[j, c][:, :1]
+            before = peak_kept[j, c, rows][:, :1]
             peak = jnp.maximum(peak, before)
             fade = jnp.exp2(before - peak)
-            total, mixture = total_kept[j, c] * fade, mixture_kept[j, c] * fade
+            total, mixture = total_kept[j, c, rows] * fade, mixture_kept[j, c, rows] * fade
+        if ready is not None:
+            ready()
         for o, see, s in zip(offsets, seen, scores):
             shift = jnp.where(see[:, :1], peak, SHUT)
             p = jnp.exp2(s * scale - shift)
@@ -228,9 +237,9 @@
     spans = [(0, early), (half * HD, half * HD + early)]
     rest = [(early, half * HD), (half * HD + early, 2 * half * HD)]
 
-    def project(pieces, cols):
+    def project(pieces, cols, rows=slice(None)):
         return sum(
-            jnp.dot(done[:, a:b], w_held[a:b, cols], preferred_element_type=jnp.float32) for a, b in pieces
+            jnp.dot(done[rows, a:b], w_held[a:b, cols], preferred_element_type=jnp.float32) for a, b in pieces
         )
 
     @pl.loop(0, half)
@@ -289,34 +298,41 @@
                 for i in range(PIECES):
                     w_sibling(k, i).wait()
             for e in range(half - 2):
-                back(e).wait_recv()
+                for r in range(PARTS):
+                    back(e, r).wait_recv()
 
             @pl.loop(0, out_ref.shape[2] // BLOCK)
             def _(n):
                 cols = pl.ds(pl.multiple_of(n * BLOCK, BLOCK), BLOCK)
                 partial[:, cols] = project(spans, cols)
 
-        @pl.when(has_down)
-        def _():
-            for copy in pass_on(c, 0):
-                copy.wait_recv()
-
-        @pl.when(has_up)
-        def _():
-            for copy in pass_on(c, 1):
-                copy.wait_recv()
-
-        stage[c] = attend(c, 1 - side, [0, 4], False)
-        back(c).start()
+        def landed(which):
+            @pl.when(has_down)
+            def _():
+                pass_on(c, 0)[which].wait_recv()
+
+            @pl.when(has_up)
+            def _():
+                pass_on(c, 1)[which].wait_recv()
+
+        landed(0)
+        for r in range(PARTS):
+            rows = slice(r * part_rows, (r + 1) * part_rows)
+            stage[c, rows] = attend(
+                c, 1 - side, [0, 4], False, rows, functools.partial(landed, 1) if r == 0 else None
+            )
+            back(c, r).start()
         head(side, c)[...] = attend(c, side, [1 + 2 * side], False)
 
-    for e in range(half - 2, half):
-        back(e).wait_recv()
-
-    @pl.loop(0, out_ref.shape[2] // BLOCK)
-    def _(n):
-        cols = pl.ds(pl.multiple_of(n * BLOCK, BLOCK), BLOCK)
-        out_ref[0, :, cols] = (partial[:, cols] + project(rest, cols)).astype(jnp.bfloat16)
+    for r in range(PARTS):
+        rows = slice(r * part_rows, (r + 1) * part_rows)
+        for e in range(half - 2, half):
+            back(e, r).wait_recv()
+
+        @pl.loop(0, out_ref.shape[2] // BLOCK)
+        def _(n):
+            cols = pl.ds(pl.multiple_of(n * BLOCK, BLOCK), BLOCK)
+            out_ref[0, rows, cols] = (partial[rows, cols] + project(rest, cols, rows)).astype(jnp.bfloat16)
 
     @pl.loop(0, half)
     def _(c):
@@ -333,7 +349,8 @@
             for copy in own_out(c, 1) + pass_on(c, 1):
                 copy.wait_send()
 
-        back(c).wait_send()
+        for r in range(PARTS):
+            back(c, r).wait_send()
 
     for k in range(1, chips):
         for i in range(PIECES):
@@ -385,8 +402,8 @@
             dma((2, 2, half)),
             dma((2, 2, half)),
             dma((2, 2, 2, half)),
-            dma((half,)),
-            dma((half,)),
+            dma((half, PARTS)),
+            dma((half, PARTS)),
         ],
         compiler_params=pltpu.CompilerParams(
             collective_id=0, has_side_effects=True, vmem_limit_bytes=60 * 1024 * 1024

time: 67.8 us -> 68.5 us (1.010)
  no operation moved by 1% of the time
where the time goes in v6:
time: 68.5 us; the launch traced here: 68.3 us
  Pallas kernels  66.6 us (97%)
  local copies, waits for them, and re-layouts  1.02 us (1%)
    pallas_call x1, Pallas kernels, per_device(): pl.pallas_call(functools.partial(kernel, tiles, shards), out_shape=pltpu....  66.6 us

profile of v6, /device:TPU:0, one launch (start us, length us, event | category | flops | bytes accessed | tf_op | source)
XLA Modules:
  0.0 68.3 jit_solution(4435359096243697390)
XLA Ops:
  0.7 66.6 %shard_map.64 = bf16[1,384,1536]{2,1,0:T(8,128)(2,1)S(1)} custom-call(bf16[1,384,1536]{2,1,0:T(8,128)(2,1)} %q_ref.1, bf16[1,384,1536]{2,1,0:T(8,128)(2,1)} %k_ref.1, bf16[1,384,1536]{2,1,0:T(8,128)(2,1)} %v_ref.1, s32[1,1,5]{2,1,0:T(1,128)} %lists_ref.1, s32[1,1]{1,0:T(1,128)S(6)} %copy.9.counts_ref, bf16[384,1536]{1,0:T(8,128)(2,1)} %w_ref.1), custom_call_target="tpu_custom_call" | custom-call | flops 4529848320 | bytes 60000000 | tf_op jit(solution)/shard_map/pallas_call | solution.py:373
  67.3 1.0 %copy.8 = bf16[1,384,1536]{2,1,0:T(8,128)(2,1)} copy(bf16[1,384,1536]{2,1,0:T(8,128)(2,1)S(1)} %shard_map.64) | data formatting | bytes 2359296

commit v7 on v5

--- a/solution.py
+++ b/solution.py
@@ -16,6 +16,7 @@
 SHUT = 1e30
 BLOCK = 256
 PIECES = 3
+AHEAD = 2
 
 
 def kernel(tiles, shards, q_ref, k_ref, v_ref, lists_ref, counts_ref, w_ref, out_ref,
@@ -224,17 +225,21 @@
         total = jnp.sum(total, axis=1, keepdims=True)
         return (mixture / total).astype(jnp.bfloat16)
 
-    early = (half - 2) * HD
-    spans = [(0, early), (half * HD, half * HD + early)]
-    rest = [(early, half * HD), (half * HD + early, 2 * half * HD)]
-
-    def project(pieces, cols):
-        return sum(
-            jnp.dot(done[:, a:b], w_held[a:b, cols], preferred_element_type=jnp.float32) for a, b in pieces
-        )
-
-    @pl.loop(0, half)
-    def _(c):
+    third = half // 3
+
+    def project(part, cols):
+        total = None
+        for a in (part * third * HD, (half + part * third) * HD):
+            b = a + third * HD
+            product = jnp.dot(done[:, a:b], w_held[a:b, cols], preferred_element_type=jnp.float32)
+            total = product if total is None else total + product
+        return total
+
+    def returned(part):
+        for e in range(part * third, (part + 1) * third):
+            back(e).wait_recv()
+
+    def forward(c):
         for copy in from_pair(c)[:2]:
             copy.wait_recv()
         to_pair(c)[2].start()
@@ -249,6 +254,15 @@
             for copy in pass_on(c, 1):
                 copy.start()
 
+    for c in range(AHEAD):
+        forward(c)
+
+    @pl.loop(0, half)
+    def _(c):
+        @pl.when(c + AHEAD < half)
+        def _():
+            forward(c + AHEAD)
+
         @pl.when(c < PIECES)
         def _():
             for k in range(1, chips):
@@ -276,25 +290,26 @@
         from_pair(c)[2].wait_recv()
         attend(c, 1 - side, [1, 2, 3], True)
 
+    @pl.loop(0, half)
+    def _(c):
         @pl.when(c < PIECES)
         def _():
             for k in range(1, chips):
                 w_chip(k, c).wait_recv()
                 w_sibling(k, c).start()
 
-        @pl.when(c == half - 1)
+        @pl.when(c == half - third)
         def _():
             w_in.wait()
             for k in range(chips):
                 for i in range(PIECES):
                     w_sibling(k, i).wait()
-            for e in range(half - 2):
-                back(e).wait_recv()
+            returned(0)
 
             @pl.loop(0, out_ref.shape[2] // BLOCK)
             def _(n):
                 cols = pl.ds(pl.multiple_of(n * BLOCK, BLOCK), BLOCK)
-                partial[:, cols] = project(spans, cols)
+                partial[:, cols] = project(0, cols)
 
         @pl.when(has_down)
         def _():
@@ -310,13 +325,19 @@
         back(c).start()
         head(side, c)[...] = attend(c, side, [1 + 2 * side], False)
 
-    for e in range(half - 2, half):
-        back(e).wait_recv()
+    returned(1)
 
     @pl.loop(0, out_ref.shape[2] // BLOCK)
     def _(n):
         cols = pl.ds(pl.multiple_of(n * BLOCK, BLOCK), BLOCK)
-        out_ref[0, :, cols] = (partial[:, cols] + project(rest, cols)).astype(jnp.bfloat16)
+        partial[:, cols] += project(1, cols)
+
+    returned(2)
+
+    @pl.loop(0, out_ref.shape[2] // BLOCK)
+    def _(n):
+        cols = pl.ds(pl.multiple_of(n * BLOCK, BLOCK), BLOCK)
+        out_ref[0, :, cols] = (partial[:, cols] + project(2, cols)).astype(jnp.bfloat16)
 
     @pl.loop(0, half)
     def _(c):

time: 67.8 us -> 65.8 us (0.971)
  Pallas kernels: 66 us -> 64 us
    pallas_call x1, Pallas kernels: 66 us -> 64 us  [per_device(): pl.pallas_call(functools.partial(kernel, tiles, shards), out_shape=pltpu....]
where the time goes in v7:
time: 65.8 us; the launch traced here: 65.7 us
  Pallas kernels  64 us (97%)
  local copies, waits for them, and re-layouts  1.02 us (2%)
  between operations  0.66 us (1%)
    pallas_call x1, Pallas kernels, per_device(): pl.pallas_call(functools.partial(kernel, tiles, shards), out_shape=pltpu....  64 us

profile of v7, /device:TPU:0, one launch (start us, length us, event | category | flops | bytes accessed | tf_op | source)
XLA Modules:
  0.0 65.7 jit_solution(479582915401955044)
XLA Ops:
  0.7 64.0 %shard_map.64 = bf16[1,384,1536]{2,1,0:T(8,128)(2,1)S(1)} custom-call(bf16[1,384,1536]{2,1,0:T(8,128)(2,1)} %q_ref.1, bf16[1,384,1536]{2,1,0:T(8,128)(2,1)} %k_ref.1, bf16[1,384,1536]{2,1,0:T(8,128)(2,1)} %v_ref.1, s32[1,1,5]{2,1,0:T(1,128)} %lists_ref.1, s32[1,1]{1,0:T(1,128)S(6)} %copy.9.counts_ref, bf16[384,1536]{1,0:T(8,128)(2,1)} %w_ref.1), custom_call_target="tpu_custom_call" | custom-call | flops 4529848320 | bytes 60000000 | tf_op jit(solution)/shard_map/pallas_call | solution.py:377
  64.7 1.0 %copy.8 = bf16[1,384,1536]{2,1,0:T(8,128)(2,1)} copy(bf16[1,384,1536]{2,1,0:T(8,128)(2,1)S(1)} %shard_map.64) | data formatting | bytes 2359296

commit v8 on v7

--- a/solution.py
+++ b/solution.py
@@ -304,6 +304,9 @@
             for k in range(chips):
                 for i in range(PIECES):
                     w_sibling(k, i).wait()
+                    if k > 0:
+                        w_chip(k, i).wait_send()
+            vis_out.wait_send()
             returned(0)
 
             @pl.loop(0, out_ref.shape[2] // BLOCK)
@@ -325,6 +328,33 @@
         back(c).start()
         head(side, c)[...] = attend(c, side, [1 + 2 * side], False)
 
+        for copy in to_pair(c):
+            copy.wait_send()
+
+        @pl.when(has_up)
+        def _():
+            for copy in own_out(c, 0):
+                copy.wait_send()
+
+        @pl.when(has_down)
+        def _():
+            for copy in own_out(c, 1):
+                copy.wait_send()
+
+        @pl.when(has_up & (c > 0))
+        def _():
+            for copy in pass_on(c - 1, 0):
+                copy.wait_send()
+
+        @pl.when(has_down & (c > 0))
+        def _():
+            for copy in pass_on(c - 1, 1):
+                copy.wait_send()
+
+        @pl.when(c > 0)
+        def _():
+            back(c - 1).wait_send()
+
     returned(1)
 
     @pl.loop(0, out_ref.shape[2] // BLOCK)
@@ -339,27 +369,17 @@
         cols = pl.ds(pl.multiple_of(n * BLOCK, BLOCK), BLOCK)
         out_ref[0, :, cols] = (partial[:, cols] + project(2, cols)).astype(jnp.bfloat16)
 
-    @pl.loop(0, half)
-    def _(c):
-        for copy in to_pair(c):
+    @pl.when(has_up)
+    def _():
+        for copy in pass_on(half - 1, 0):
             copy.wait_send()
 
-        @pl.when(has_up)
-        def _():
-            for copy in own_out(c, 0) + pass_on(c, 0):
-                copy.wait_send()
-
-        @pl.when(has_down)
-        def _():
-            for copy in own_out(c, 1) + pass_on(c, 1):
-                copy.wait_send()
-
-        back(c).wait_send()
-
-    for k in range(1, chips):
-        for i in range(PIECES):
-            w_chip(k, i).wait_send()
-    vis_out.wait_send()
+    @pl.when(has_down)
+    def _():
+        for copy in pass_on(half - 1, 1):
+            copy.wait_send()
+
+    back(half - 1).wait_send()
 
 
 def per_device(queries, key_rows, value_rows, tile_lists, tile_counts, out_weight):

time: 65.8 us -> 65.7 us (level)
  no operation moved by 1% of the time
where the time goes in v8:
time: 65.7 us; the launch traced here: 65.6 us
  Pallas kernels  63.9 us (97%)
  local copies, waits for them, and re-layouts  1.02 us (2%)
  between operations  0.66 us (1%)
    pallas_call x1, Pallas kernels, per_device(): pl.pallas_call(functools.partial(kernel, tiles, shards), out_shape=pltpu....  63.9 us

profile of v8, /device:TPU:0, one launch (start us, length us, event | category | flops | bytes accessed | tf_op | source)
XLA Modules:
  0.0 65.6 jit_solution(9333796178674033779)
XLA Ops:
  0.7 63.9 %shard_map.64 = bf16[1,384,1536]{2,1,0:T(8,128)(2,1)S(1)} custom-call(bf16[1,384,1536]{2,1,0:T(8,128)(2,1)} %q_ref.1, bf16[1,384,1536]{2,1,0:T(8,128)(2,1)} %k_ref.1, bf16[1,384,1536]{2,1,0:T(8,128)(2,1)} %v_ref.1, s32[1,1,5]{2,1,0:T(1,128)} %lists_ref.1, s32[1,1]{1,0:T(1,128)S(6)} %copy.9.counts_ref, bf16[384,1536]{1,0:T(8,128)(2,1)} %w_ref.1), custom_call_target="tpu_custom_call" | custom-call | flops 4529848320 | bytes 60000000 | tf_op jit(solution)/shard_map/pallas_call | solution.py:397
  64.6 1.0 %copy.8 = bf16[1,384,1536]{2,1,0:T(8,128)(2,1)} copy(bf16[1,384,1536]{2,1,0:T(8,128)(2,1)S(1)} %shard_map.64) | data formatting | bytes 2359296

commit v9 on v8

--- a/solution.py
+++ b/solution.py
@@ -14,7 +14,7 @@
 WINDOW = 6
 HIDDEN = -1e30
 SHUT = 1e30
-BLOCK = 256
+BLOCK = 512
 PIECES = 3
 AHEAD = 2
 
@@ -192,10 +192,13 @@
     def attend(c, j, offsets, first):
         q = q_held[j, c]
         seen = [vis_held[j, pl.ds(o, 1), :] > 0.0 for o in offsets]
-        scores, peak = [], None
-        for o, see in zip(offsets, seen):
-            s = lax.dot_general(q, k_held[j + o, c], (((1,), (1,)), ((), ())), preferred_element_type=jnp.float32)
-            scores.append(s)
+        keys = jnp.concatenate([k_held[j + o, c] for o in offsets], axis=0)
+        values = jnp.concatenate([v_held[j + o, c] for o in offsets], axis=0)
+        every = lax.dot_general(q, keys, (((1,), (1,)), ((), ())), preferred_element_type=jnp.float32)
+        wide = k_held.shape[2]
+        scores = [every[:, i * wide : (i + 1) * wide] for i in range(len(offsets))]
+        peak = None
+        for see, s in zip(seen, scores):
             top = s[:, :HD]
             for lane in range(HD, s.shape[1], HD):
                 top = jnp.maximum(top, s[:, lane : lane + HD])
@@ -209,14 +212,16 @@
             peak = jnp.maximum(peak, before)
             fade = jnp.exp2(before - peak)
             total, mixture = total_kept[j, c] * fade, mixture_kept[j, c] * fade
-        for o, see, s in zip(offsets, seen, scores):
+        probs = []
+        for see, s in zip(seen, scores):
             shift = jnp.where(see[:, :1], peak, SHUT)
             p = jnp.exp2(s * scale - shift)
             for lane in range(0, p.shape[1], HD):
                 part = p[:, lane : lane + HD]
                 total = part if total is None else total + part
-            part = jnp.dot(p.astype(jnp.bfloat16), v_held[j + o, c], preferred_element_type=jnp.float32)
-            mixture = part if mixture is None else mixture + part
+            probs.append(p.astype(jnp.bfloat16))
+        product = jnp.dot(jnp.concatenate(probs, axis=1), values, preferred_element_type=jnp.float32)
+        mixture = product if mixture is None else mixture + product
         if first:
             peak_kept[j, c] = jnp.broadcast_to(peak, mixture.shape)
             total_kept[j, c] = total
@@ -228,12 +233,10 @@
     third = half // 3
 
     def project(part, cols):
-        total = None
-        for a in (part * third * HD, (half + part * third) * HD):
-            b = a + third * HD
-            product = jnp.dot(done[:, a:b], w_held[a:b, cols], preferred_element_type=jnp.float32)
-            total = product if total is None else total + product
-        return total
+        starts = (part * third * HD, (half + part * third) * HD)
+        left = jnp.concatenate([done[:, a : a + third * HD] for a in starts], axis=1)
+        right = jnp.concatenate([w_held[a : a + third * HD, cols] for a in starts], axis=0)
+        return jnp.dot(left, right, preferred_element_type=jnp.float32)
 
     def returned(part):
         for e in range(part * third, (part + 1) * third):

time: 65.7 us -> 65.4 us (level)
  no operation moved by 1% of the time
where the time goes in v9:
time: 65.4 us; the launch traced here: 65.3 us
  Pallas kernels  63.6 us (97%)
  local copies, waits for them, and re-layouts  1.02 us (2%)
  between operations  0.66 us (1%)
    pallas_call x1, Pallas kernels, per_device(): pl.pallas_call(functools.partial(kernel, tiles, shards), out_shape=pltpu....  63.6 us

profile of v9, /device:TPU:0, one launch (start us, length us, event | category | flops | bytes accessed | tf_op | source)
XLA Modules:
  0.0 65.3 jit_solution(6562278980865338409)
XLA Ops:
  0.7 63.6 %shard_map.64 = bf16[1,384,1536]{2,1,0:T(8,128)(2,1)S(1)} custom-call(bf16[1,384,1536]{2,1,0:T(8,128)(2,1)} %q_ref.1, bf16[1,384,1536]{2,1,0:T(8,128)(2,1)} %k_ref.1, bf16[1,384,1536]{2,1,0:T(8,128)(2,1)} %v_ref.1, s32[1,1,5]{2,1,0:T(1,128)} %lists_ref.1, s32[1,1]{1,0:T(1,128)S(6)} %copy.9.counts_ref, bf16[384,1536]{1,0:T(8,128)(2,1)} %w_ref.1), custom_call_target="tpu_custom_call" | custom-call | flops 4529848320 | bytes 60000000 | tf_op jit(solution)/shard_map/pallas_call | solution.py:400
  64.3 1.0 %copy.8 = bf16[1,384,1536]{2,1,0:T(8,128)(2,1)} copy(bf16[1,384,1536]{2,1,0:T(8,128)(2,1)S(1)} %shard_map.64) | data formatting | bytes 2359296

commit v10 on v9

--- a/solution.py
+++ b/solution.py
@@ -16,7 +16,7 @@
 SHUT = 1e30
 BLOCK = 512
 PIECES = 3
-AHEAD = 2
+AHEAD = 3
 
 
 def kernel(tiles, shards, q_ref, k_ref, v_ref, lists_ref, counts_ref, w_ref, out_ref,

time: 65.4 us -> 66 us (level)
  no operation moved by 1% of the time
where the time goes in v10:
time: 66 us; the launch traced here: 65.9 us
  Pallas kernels  64.2 us (97%)
  local copies, waits for them, and re-layouts  1.02 us (2%)
  between operations  0.66 us (1%)
    pallas_call x1, Pallas kernels, per_device(): pl.pallas_call(functools.partial(kernel, tiles, shards), out_shape=pltpu....  64.2 us

profile of v10, /device:TPU:0, one launch (start us, length us, event | category | flops | bytes accessed | tf_op | source)
XLA Modules:
  0.0 65.9 jit_solution(12023724902401270472)
XLA Ops:
  0.7 64.2 %shard_map.64 = bf16[1,384,1536]{2,1,0:T(8,128)(2,1)S(1)} custom-call(bf16[1,384,1536]{2,1,0:T(8,128)(2,1)} %q_ref.1, bf16[1,384,1536]{2,1,0:T(8,128)(2,1)} %k_ref.1, bf16[1,384,1536]{2,1,0:T(8,128)(2,1)} %v_ref.1, s32[1,1,5]{2,1,0:T(1,128)} %lists_ref.1, s32[1,1]{1,0:T(1,128)S(6)} %copy.9.counts_ref, bf16[384,1536]{1,0:T(8,128)(2,1)} %w_ref.1), custom_call_target="tpu_custom_call" | custom-call | flops 4529848320 | bytes 60000000 | tf_op jit(solution)/shard_map/pallas_call | solution.py:400
  64.8 1.0 %copy.8 = bf16[1,384,1536]{2,1,0:T(8,128)(2,1)} copy(bf16[1,384,1536]{2,1,0:T(8,128)(2,1)S(1)} %shard_map.64) | data formatting | bytes 2359296
